TPU v7x, 512 devices: a whole 4x4x16 slice. The times are simulated.
512 devices in a mesh: depth: 128 (over z, x, core), head: 4 (over y).
Axes of the slice: x: 4, y: 4, z: 16, core: 2. Of those that a mesh axis runs over, the one named last changes fastest.
Arguments:
- queries: bfloat16 [1536, 768, 256], P('depth', 'head'), may hold values from -8 to 8
- keys: bfloat16 [1536, 768, 256], P('depth', 'head'), may hold values from -6 to 6
- values: bfloat16 [1536, 768, 256], P('depth', 'head'), may hold values from -6 to 6
- w_out: bfloat16 [768, 768], P('head'), may hold values from -0.21875 to 0.21875
Outputs:
- mixed: bfloat16 [1536, 768, 256], P('depth', 'head')
All inputs are finite; a program needn't handle non-finite values.
Results may differ from a plain program's by a relative error of at most 0.0057.
Values may be sent and summed in bfloat16 or wider, within the bound.
A program may use at most 64 MiB of HBM per device.

v0:
```python
import math

import jax
import jax.numpy as jnp
from jax import lax
from jax.sharding import PartitionSpec as P

HEAD_DIM = 64


def per_device(queries, keys, values, w_out):
    rows_here, local_width, columns = queries.shape
    local_heads = local_width // HEAD_DIM
    scaling = 1.0 / math.sqrt(HEAD_DIM * rows_here * lax.axis_size("depth"))
    query_heads = queries.reshape(rows_here, local_heads, HEAD_DIM, columns)
    key_heads = keys.reshape(rows_here, local_heads, HEAD_DIM, columns)
    value_heads = values.reshape(rows_here, local_heads, HEAD_DIM, columns)
    partial_sum = jnp.einsum(
        "rhei,rhej->ihj", query_heads, key_heads, preferred_element_type=jnp.float32
    )
    summed = lax.psum(partial_sum, "depth")
    probs = jax.nn.softmax(summed * scaling, axis=-1).astype(jnp.bfloat16)
    attended = jnp.einsum("ihj,rhej->rhei", probs, value_heads, preferred_element_type=jnp.float32)
    attended = attended.astype(jnp.bfloat16).reshape(rows_here, local_width, columns)
    mixed = jnp.einsum(
        "dc,rci->rdi",
        w_out,
        lax.all_gather(attended, "head", axis=1, tiled=True),
        preferred_element_type=jnp.float32,
    )
    return mixed.astype(jnp.bfloat16)


def solution(mesh):
    return jax.shard_map(
        per_device,
        mesh=mesh,
        in_specs=(
            P("depth", "head", None),
            P("depth", "head", None),
            P("depth", "head", None),
            P("head", None),
        ),
        out_specs=P("depth", "head", None),
        check_vma=False,
    )
```

profile of v0, /device:TPU:1, one launch (start us, length us, event | category | flops | bytes accessed | tf_op | source)
XLA Modules:
  0.0 422.0 jit_solution(14321368145300847875)
XLA Ops:
  6.5 0.0 copy-start
  6.5 0.0 all-reduce.2.cloned.1.call-start
  6.5 3.1 convolution_bitcast_fusion
  9.7 0.0 all-reduce.2.cloned.1.call-update
  9.7 0.0 all-gather.2.cloned.1.call-start
  9.7 338.7 %all-reduce.2.cloned.1.call-done = f32[256,3,256]{0,2,1:T(8,128)} async-done(((f32[256,3,256]{0,2,1:T(8,128)}), f32[256,3,256]{0,2,1:T(8,128)}) %all-reduce.2.cloned.1.call-update) | async-done | bytes 786448 | tf_op jit(solution)/shard_map/psum | solution.py:21
  348.4 1.4 fusion.18
  349.8 0.0 copy-done
  349.8 1.7 fusion.1
  351.5 1.1 copy.13
  352.6 0.0 copy-start.1
  352.6 0.0 all-gather.2.cloned.1.call-update
  352.6 58.1 %all-gather.2.cloned.1.call-done = bf16[12,768,256]{2,1,0:T(8,128)(2,1)} async-done(((bf16[12,192,256]{2,1,0:T(8,128)(2,1)}), bf16[12,768,256]{2,1,0:T(8,128)(2,1)}) %all-gather.2.cloned.1.call-update) | async-done | bytes 4718608 | tf_op jit(solution)/shard_map/all_gather | solution.py:28
  410.7 0.0 copy-done.1
  410.7 4.4 %fusion.3 = bf16[12,192,256]{2,1,0:T(8,128)(2,1)} fusion(bf16[12,768,256]{2,1,0:T(8,128)(2,1)} %all-gather.2.cloned.1.call-done, bf16[192,768]{1,0:T(8,128)(2,1)S(1)} %copy-done.1), kind=kOutput, calls=%fused_computation.5 | convolution fusion | flops 906559488 | bytes 6193152 | tf_op jit(solution)/shard_map/dc,rci->rdi/dot_general | solution.py:25
Async XLA Ops:
  6.5 343.3 %copy-start = (bf16[12,192,256]{2,1,0:T(8,128)(2,1)S(1)}, bf16[12,192,256]{2,1,0:T(8,128)(2,1)}, u32[]{:S(2)}) copy-start(bf16[12,192,256]{2,1,0:T(8,128)(2,1)} %param.6) | copy-start | bytes 3538948
  6.5 341.9 %all-reduce.2.cloned.1.call-start = ((), (), s32[]{:S(2)}) async-start(), calls=%async_computation | async-start | bytes 1572864 | tf_op jit(solution)/shard_map/psum | solution.py:21
  9.7 401.0 %all-gather.2.cloned.1.call-start = ((), (), s32[]{:S(2)}) async-start(), calls=%async_computation.1 | async-start | bytes 5898240 | tf_op jit(solution)/shard_map/all_gather | solution.py:28
  352.6 58.1 %copy-start.1 = (bf16[192,768]{1,0:T(8,128)(2,1)S(1)}, bf16[192,768]{1,0:T(8,128)(2,1)}, u32[]{:S(2)}) copy-start(bf16[192,768]{1,0:T(8,128)(2,1)} %param.7) | copy-start | bytes 884740
Sparse Core Ops, SparseCore 0:
  10.8 337.5 all-reduce.1
  352.8 57.9 all-gather.1
where the time goes:
time: 422 us
  waiting for transfers between devices  397 us (94%)
  between operations  13.4 us (3%)
  matrix products  9.28 us (2%)
    psum x1, waiting for transfers between devices, per_device(): summed = lax.psum(partial_sum, 'depth')  339 us
    all_gather x1, waiting for transfers between devices, per_device(): lax.all_gather(attended, 'head', axis=1, tiled=True)  58.1 us
  transfers between devices with their start and end apart: 2, of which 2 were waited for; matrix products, arithmetic and copies ran while one was open for 0% of the time, Pallas kernels for 0%

commit v1 on v0

v1 whole, which is shorter than its diff:
```python
import math

import jax
import jax.numpy as jnp
from jax import lax
from jax.experimental import pallas as pl
from jax.experimental.pallas import tpu as pltpu
from jax.sharding import PartitionSpec as P

HEAD_DIM = 64
NZ, NX, NY, NC = 16, 4, 4, 2
LOCAL_HEADS = 3
ROWS_HERE = 12
WIDTH_HERE = LOCAL_HEADS * HEAD_DIM
COLS = 256
HALF = COLS // NC
XROWS = HALF // NX
GROUPS = XROWS // 8
HALF_SEQ = ROWS_HERE // 2
SCALING = 1.0 / math.sqrt(HEAD_DIM * ROWS_HERE * NZ * NX * NC)
MESH = pl.DeviceIdType.MESH


def kernel(
    q_hbm, k_hbm, v_hbm, w_hbm, out_hbm,
    q_v, k_v, vals, w_v, part, c_recv, csum, x_recv, xsum, z_recv, pg, zg, probs, att, out_v,
    load_sem, v_ssem, v_rsem, c_ssem, c_rsem, x_ssem, x_rsem, z_ssem, z_rsem,
    y_ssem, y_rsem, zg_ssem, zg_rsem, xg_ssem, xg_rsem, cg_ssem, cg_rsem, out_sem,
):
    me = lax.axis_index("depth")
    y = lax.axis_index("head")
    core = lax.rem(me, NC)
    x = lax.rem(me // NC, NX)
    z = me // (NC * NX)

    def at(z=z, x=x, core=core, y=y):
        return ((z * NX + x) * NC + core, y)

    def turn(index, by, size):
        return lax.rem(index + by, size)

    def send(src, dst, ssem, rsem, device):
        copy = pltpu.make_async_remote_copy(
            src_ref=src, dst_ref=dst, send_sem=ssem, recv_sem=rsem,
            device_id=device, device_id_type=MESH,
        )
        copy.start()
        return copy

    def arrived(dst, sem):
        pltpu.make_async_remote_copy(
            src_ref=dst, dst_ref=dst, send_sem=sem, recv_sem=sem,
            device_id=at(), device_id_type=MESH,
        ).wait_recv()

    mate = at(core=1 - core)
    barrier = pltpu.get_barrier_semaphore()
    partners = (
        [at(y=turn(y, d, NY)) for d in range(1, NY)]
        + [mate]
        + [at(x=turn(x, d, NX)) for d in range(1, NX)]
        + [at(z=turn(z, d, NZ)) for d in range(1, NZ)]
    )
    for partner in partners:
        pl.semaphore_signal(barrier, inc=1, device_id=partner, device_id_type=MESH)

    loads = []
    for h in range(LOCAL_HEADS):
        features = pl.ds(h * HEAD_DIM, HEAD_DIM)
        pair = (
            pltpu.make_async_copy(q_hbm.at[:, features, :], q_v.at[h], load_sem.at[2 * h]),
            pltpu.make_async_copy(k_hbm.at[:, features, :], k_v.at[h], load_sem.at[2 * h + 1]),
        )
        for copy in pair:
            copy.start()
        loads.append(pair)
    load_v = pltpu.make_async_copy(v_hbm, vals.at[y], load_sem.at[2 * LOCAL_HEADS])
    load_v.start()
    load_w = pltpu.make_async_copy(w_hbm, w_v, load_sem.at[2 * LOCAL_HEADS + 1])
    load_w.start()

    started = []

    def partial_logits(h):
        for copy in loads[h]:
            copy.wait()
        part[h] = lax.dot_general(
            q_v[h].reshape(ROWS_HERE * HEAD_DIM, COLS),
            k_v[h].reshape(ROWS_HERE * HEAD_DIM, COLS),
            (((0,), (0,)), ((), ())),
            preferred_element_type=jnp.float32,
        )

    def to_mate(h):
        theirs = pl.ds(pl.multiple_of((1 - core) * HALF, HALF), HALF)
        started.append(send(part.at[h, theirs], c_recv.at[h], c_ssem.at[h], c_rsem.at[h], mate))

    partial_logits(0)
    pl.semaphore_wait(barrier, len(partners))
    to_mate(0)

    left, right, far = turn(y, NY - 1, NY), turn(y, 1, NY), turn(y, 2, NY)
    first, second = pl.ds(0, HALF_SEQ), pl.ds(HALF_SEQ, HALF_SEQ)
    for number, (rows, target) in enumerate(
        ((first, right), (second, left), (second, right), (first, left))
    ):
        started.append(send(
            v_hbm.at[rows], vals.at[y, rows], v_ssem.at[number], v_rsem.at[number], at(y=target)
        ))

    for h in range(1, LOCAL_HEADS):
        partial_logits(h)
        to_mate(h)

    ours = pl.ds(pl.multiple_of(core * HALF, HALF), HALF)
    for h in range(LOCAL_HEADS):
        arrived(c_recv.at[h], c_rsem.at[h])
        csum[h] = (part[h, ours, :] + c_recv[h]).reshape(NX, XROWS, COLS)
        for d in range(1, NX):
            other = turn(x, d, NX)
            started.append(send(
                csum.at[h, other], x_recv.at[h, x], x_ssem.at[h, d], x_rsem.at[h, x], at(x=other)
            ))

    for h in range(LOCAL_HEADS):
        total = csum[h, x]
        for d in range(1, NX):
            other = turn(x, d, NX)
            arrived(x_recv.at[h, other], x_rsem.at[h, other])
            total = total + x_recv[h, other]
        xsum[h] = total.reshape(GROUPS, 8, COLS)
        for t in range(GROUPS):
            owner = lax.rem(t * 4 + h + NZ - 2 * core, NZ)

            @pl.when(owner != z)
            def _():
                send(
                    xsum.at[h, t], z_recv.at[z], z_ssem.at[h, t], z_rsem.at[z], at(z=owner)
                )

            @pl.when(owner == z)
            def _():
                z_recv[z] = xsum[h, t]

    turned = turn(z, 2 * core, NZ)
    own_head, own_group = lax.rem(turned, 4), turned // 4

    @pl.when(own_head < LOCAL_HEADS)
    def _():
        for d in range(1, NZ):
            other = turn(z, d, NZ)
            arrived(z_recv.at[other], z_rsem.at[other])
        logits = jnp.sum(z_recv[...], axis=0) * SCALING
        top = jnp.max(logits, axis=-1, keepdims=True)
        powers = jnp.exp(logits - top)
        p = powers / jnp.sum(powers, axis=-1, keepdims=True)
        pg[y] = jnp.concatenate([p[:, :128], p[:, 128:]], axis=0).astype(jnp.bfloat16)
        copies = [
            send(pg.at[y], pg.at[y], y_ssem.at[d], y_rsem.at[y], at(y=turn(y, d, NY)))
            for d in range(1, NY)
        ]
        for d in range(1, NY):
            other = turn(y, d, NY)
            arrived(pg.at[other], y_rsem.at[other])
        mine = own_head * GROUPS + own_group
        for d in range(1, NZ):
            copies.append(send(
                pg, zg.at[mine], zg_ssem.at[d], zg_rsem.at[mine], at(z=turn(z, d, NZ))
            ))
        zg[mine] = pg[...]
        for copy in copies:
            copy.wait_send()

    arrived(vals.at[left, first], v_rsem.at[0])
    started.append(send(
        vals.at[left, first], vals.at[left, first], v_ssem.at[4], v_rsem.at[4], at(y=right)
    ))
    arrived(vals.at[right, second], v_rsem.at[1])
    started.append(send(
        vals.at[right, second], vals.at[right, second], v_ssem.at[5], v_rsem.at[5], at(y=left)
    ))

    here = core * NX + x
    for h in range(LOCAL_HEADS):
        for t in range(GROUPS):
            number = h * GROUPS + t
            owner = lax.rem(t * 4 + h + NZ - 2 * core, NZ)

            @pl.when(owner != z)
            def _():
                arrived(zg.at[number], zg_rsem.at[number])

        for other_y in range(NY):
            blocks = []
            for t in range(GROUPS):
                block = zg[h * GROUPS + t, other_y].astype(jnp.float32)
                blocks.append(jnp.concatenate([block[:8], block[8:]], axis=1))
            probs[h, other_y, here] = jnp.concatenate(blocks, axis=0).astype(jnp.bfloat16)
        for d in range(1, NX):
            started.append(send(
                probs.at[h, :, here], probs.at[h, :, here],
                xg_ssem.at[h, d], xg_rsem.at[h, x], at(x=turn(x, d, NX)),
            ))

    our_blocks = pl.ds(pl.multiple_of(core * NX, NX), NX)
    mate_blocks = pl.ds(pl.multiple_of((1 - core) * NX, NX), NX)
    for h in range(LOCAL_HEADS):
        for d in range(1, NX):
            other = turn(x, d, NX)
            arrived(probs.at[h, :, core * NX + other], xg_rsem.at[h, other])
        started.append(send(
            probs.at[h, :, our_blocks], probs.at[h, :, our_blocks], cg_ssem.at[h], cg_rsem.at[h], mate
        ))

    load_v.wait()
    load_w.wait()
    arrived(vals.at[right, first], v_rsem.at[3])
    arrived(vals.at[left, second], v_rsem.at[2])
    arrived(vals.at[far, first], v_rsem.at[4])
    arrived(vals.at[far, second], v_rsem.at[5])
    for h in range(LOCAL_HEADS):
        arrived(probs.at[h, :, mate_blocks], cg_rsem.at[h])
        features = pl.ds(h * HEAD_DIM, HEAD_DIM)
        for other_y in range(NY):
            attended = lax.dot_general(
                vals[other_y, :, features, :].reshape(ROWS_HERE * HEAD_DIM, COLS),
                probs[h, other_y].reshape(COLS, COLS),
                (((1,), (1,)), ((), ())),
                preferred_element_type=jnp.float32,
            )
            att[:, pl.ds(other_y * WIDTH_HERE + h * HEAD_DIM, HEAD_DIM), :] = (
                attended.astype(jnp.bfloat16).reshape(ROWS_HERE, HEAD_DIM, COLS)
            )

    for r in range(ROWS_HERE):
        out_v[r] = jnp.dot(w_v[...], att[r], preferred_element_type=jnp.float32).astype(jnp.bfloat16)
        pltpu.make_async_copy(out_v.at[r], out_hbm.at[r], out_sem.at[r]).start()
    for r in range(ROWS_HERE):
        pltpu.make_async_copy(out_v.at[r], out_hbm.at[r], out_sem.at[r]).wait()

    for copy in started:
        copy.wait_send()
    for h in range(LOCAL_HEADS):
        for t in range(GROUPS):
            owner = lax.rem(t * 4 + h + NZ - 2 * core, NZ)

            @pl.when(owner != z)
            def _():
                pltpu.make_async_remote_copy(
                    src_ref=xsum.at[h, t], dst_ref=z_recv.at[z],
                    send_sem=z_ssem.at[h, t], recv_sem=z_rsem.at[z],
                    device_id=at(z=owner), device_id_type=MESH,
                ).wait_send()


def per_device(queries, keys, values, w_out):
    f32, bf16 = jnp.float32, jnp.bfloat16
    dma = pltpu.SemaphoreType.DMA
    whole = WIDTH_HERE * NY
    any_spec = pl.BlockSpec(memory_space=pl.ANY)
    return pl.pallas_call(
        kernel,
        out_shape=jax.ShapeDtypeStruct(values.shape, bf16),
        in_specs=[any_spec] * 4,
        out_specs=any_spec,
        scratch_shapes=[
            pltpu.VMEM((LOCAL_HEADS, ROWS_HERE, HEAD_DIM, COLS), bf16),
            pltpu.VMEM((LOCAL_HEADS, ROWS_HERE, HEAD_DIM, COLS), bf16),
            pltpu.VMEM((NY, ROWS_HERE, WIDTH_HERE, COLS), bf16),
            pltpu.VMEM((WIDTH_HERE, whole), bf16),
            pltpu.VMEM((LOCAL_HEADS, COLS, COLS), f32),
            pltpu.VMEM((LOCAL_HEADS, HALF, COLS), f32),
            pltpu.VMEM((LOCAL_HEADS, NX, XROWS, COLS), f32),
            pltpu.VMEM((LOCAL_HEADS, NX, XROWS, COLS), f32),
            pltpu.VMEM((LOCAL_HEADS, GROUPS, 8, COLS), f32),
            pltpu.VMEM((NZ, 8, COLS), f32),
            pltpu.VMEM((NY, 16, 128), bf16),
            pltpu.VMEM((LOCAL_HEADS * GROUPS, NY, 16, 128), bf16),
            pltpu.VMEM((LOCAL_HEADS, NY, NC * NX, XROWS, COLS), bf16),
            pltpu.VMEM((ROWS_HERE, whole, COLS), bf16),
            pltpu.VMEM((ROWS_HERE, WIDTH_HERE, COLS), bf16),
            dma((2 * LOCAL_HEADS + 2,)),
            dma((6,)),
            dma((6,)),
            dma((LOCAL_HEADS,)),
            dma((LOCAL_HEADS,)),
            dma((LOCAL_HEADS, NX)),
            dma((LOCAL_HEADS, NX)),
            dma((LOCAL_HEADS, GROUPS)),
            dma((NZ,)),
            dma((NY,)),
            dma((NY,)),
            dma((NZ,)),
            dma((LOCAL_HEADS * GROUPS,)),
            dma((LOCAL_HEADS, NX)),
            dma((LOCAL_HEADS, NX)),
            dma((LOCAL_HEADS,)),
            dma((LOCAL_HEADS,)),
            dma((ROWS_HERE,)),
        ],
        compiler_params=pltpu.CompilerParams(
            collective_id=0, has_side_effects=True, vmem_limit_bytes=56 * 1024 * 1024
        ),
        cost_estimate=pl.CostEstimate(
            flops=3_000_000_000, bytes_accessed=5_000_000, transcendentals=2048
        ),
    )(queries, keys, values, w_out)


def solution(mesh):
    return jax.shard_map(
        per_device,
        mesh=mesh,
        in_specs=(
            P("depth", "head", None),
            P("depth", "head", None),
            P("depth", "head", None),
            P("head", None),
        ),
        out_specs=P("depth", "head", None),
        check_vma=False,
    )
```

time: 422 us -> 72.8 us (0.17)
  waiting for transfers between devices: 397 us -> 0 us
  Pallas kernels: 0 us -> 70.3 us
  between operations: 13.4 us -> 0.01 us
  matrix products: 9.28 us -> 0 us
    psum x1 -> x0, waiting for transfers between devices: 339 us -> none  [per_device(): summed = lax.psum(partial_sum, 'depth')]
    pallas_call x0 -> x1, Pallas kernels: none -> 70.3 us  [per_device(): pl.pallas_call(kernel, out_shape=jax.ShapeDtypeStruct(values.shape, bf16)...]
    all_gather x1 -> x0, waiting for transfers between devices: 58.1 us -> none  [per_device(): lax.all_gather(attended, 'head', axis=1, tiled=True)]
    dot_general x3 -> x0, matrix products: 9.28 us -> none  [the longest x1 4.44 us: per_device(): jnp.einsum('dc,rci->rdi', w_out, lax.all_gather(attended, 'head', axis=1,...]
  transfers between devices with their start and end apart: 2 -> 0, of which waited for: 2 -> 0; matrix products, arithmetic and copies ran while one was open for 0% -> 0% of each run, Pallas kernels for 0% -> 0%
where the time goes in v1:
time: 72.8 us; the launch traced here: 72.6 us
  Pallas kernels  70.3 us (97%)
  local copies, waits for them, and re-layouts  2.36 us (3%)
    pallas_call x1, Pallas kernels, per_device(): pl.pallas_call(kernel, out_shape=jax.ShapeDtypeStruct(values.shape, bf16)...  70.3 us
    unnamed x1, local copies, waits for them, and re-layouts  2.36 us

profile of v1, /device:TPU:1, one launch (start us, length us, event | category | flops | bytes accessed | tf_op | source)
XLA Modules:
  0.0 72.6 jit_solution(12718465560045137001)
XLA Ops:
  0.0 70.3 %shard_map.46 = bf16[12,192,256]{2,1,0:T(8,128)(2,1)} custom-call(bf16[12,192,256]{2,1,0:T(8,128)(2,1)} %q_hbm.1, bf16[12,192,256]{2,1,0:T(8,128)(2,1)} %k_hbm.1, bf16[12,192,256]{2,1,0:T(8,128)(2,1)} %v_hbm.1, bf16[192,768]{1,0:T(8,128)(2,1)} %w_hbm.1), custom_call_target="tpu_custom_call" | custom-call | flops 3000000000 | bytes 5000000 | tf_op jit(solution)/shard_map/pallas_call | solution.py:261
  70.3 2.4 %copy.6 = bf16[12,192,256]{2,1,0:T(8,128)(2,1)} copy(bf16[12,192,256]{2,1,0:T(8,128)(2,1)} %shard_map.46) | data formatting | bytes 2359296

commit v2 on v1

v2 whole, which is shorter than its diff:
```python
import math

import jax
import jax.numpy as jnp
from jax import lax
from jax.experimental import pallas as pl
from jax.experimental.pallas import tpu as pltpu
from jax.sharding import PartitionSpec as P

HEAD_DIM = 64
NZ, NX, NY, NC = 16, 4, 4, 2
LOCAL_HEADS = 3
ROWS_HERE = 12
WIDTH_HERE = LOCAL_HEADS * HEAD_DIM
COLS = 256
HALF = COLS // NC
XROWS = HALF // NX
GROUPS = XROWS // 8
HALF_SEQ = ROWS_HERE // 2
SCALING = 1.0 / math.sqrt(HEAD_DIM * ROWS_HERE * NZ * NX * NC)
MESH = pl.DeviceIdType.MESH


def exchange(
    q_hbm, k_hbm, v_hbm, w_hbm, att, w_v,
    q_v, k_v, vals, part, c_recv, csum, x_recv, xsum, z_recv, pg, zg, probs,
    load_sem, met_sem, v_ssem, v_rsem, c_ssem, c_rsem, x_ssem, x_rsem, z_ssem, z_rsem,
    zg_ssem, zg_rsem, z2_ssem, z2_rsem, xg_ssem, xg_rsem, cg_ssem, cg_rsem,
):
    me = lax.axis_index("depth")
    y = lax.axis_index("head")
    core = lax.rem(me, NC)
    x = lax.rem(me // NC, NX)
    z = me // (NC * NX)

    def at(z=z, x=x, core=core, y=y):
        return ((z * NX + x) * NC + core, y)

    def turn(index, by, size):
        return lax.rem(index + by, size)

    def remote(src, dst, ssem, rsem, device):
        return pltpu.make_async_remote_copy(
            src_ref=src, dst_ref=dst, send_sem=ssem, recv_sem=rsem,
            device_id=device, device_id_type=MESH,
        )

    def send(*args):
        copy = remote(*args)
        copy.start()
        return copy

    def arrived(dst, sem):
        remote(dst, dst, sem, sem, at()).wait_recv()

    mate = at(core=1 - core)
    barrier = pltpu.get_barrier_semaphore()
    near = (
        [at(y=turn(y, d, NY)) for d in range(1, NY)]
        + [mate]
        + [at(x=turn(x, d, NX)) for d in range(1, NX)]
    )
    for partner in near:
        pl.semaphore_signal(barrier, inc=1, device_id=partner, device_id_type=MESH)

    def along_z(semaphore, distance):
        @pl.when(z >= distance)
        def _():
            pl.semaphore_signal(
                semaphore, inc=1, device_id=at(z=z - distance), device_id_type=MESH
            )

        @pl.when(z + distance < NZ)
        def _():
            pl.semaphore_signal(
                semaphore, inc=1, device_id=at(z=z + distance), device_id_type=MESH
            )

    def count_z(distance):
        return jnp.where(z >= distance, 1, 0) + jnp.where(z + distance < NZ, 1, 0)

    along_z(barrier, 1)

    loads = []
    for h in range(LOCAL_HEADS):
        features = pl.ds(h * HEAD_DIM, HEAD_DIM)
        pair = (
            pltpu.make_async_copy(q_hbm.at[:, features, :], q_v.at[h], load_sem.at[2 * h]),
            pltpu.make_async_copy(k_hbm.at[:, features, :], k_v.at[h], load_sem.at[2 * h + 1]),
        )
        for copy in pair:
            copy.start()
        loads.append(pair)
    load_v = pltpu.make_async_copy(v_hbm, vals.at[y], load_sem.at[2 * LOCAL_HEADS])
    load_v.start()
    load_w = pltpu.make_async_copy(w_hbm, w_v, load_sem.at[2 * LOCAL_HEADS + 1])
    load_w.start()

    pl.semaphore_wait(barrier, len(near) + count_z(1))
    along_z(met_sem.at[0], 1)

    def meet(step):
        pl.semaphore_wait(met_sem.at[step], count_z(2**step))
        if step < 3:
            along_z(met_sem.at[step + 1], 2 ** (step + 1))

    started = []

    left, right, far = turn(y, NY - 1, NY), turn(y, 1, NY), turn(y, 2, NY)
    first, second = pl.ds(0, HALF_SEQ), pl.ds(HALF_SEQ, HALF_SEQ)

    def send_values(number, rows, target):
        started.append(send(
            v_hbm.at[rows], vals.at[y, rows], v_ssem.at[number], v_rsem.at[number], at(y=target)
        ))

    send_values(0, first, right)
    send_values(1, second, left)

    def second_hop():
        arrived(vals.at[left, first], v_rsem.at[0])
        send(vals.at[left, first], vals.at[left, first], v_ssem.at[4], v_rsem.at[4], at(y=right))
        arrived(vals.at[right, second], v_rsem.at[1])
        send(vals.at[right, second], vals.at[right, second], v_ssem.at[5], v_rsem.at[5], at(y=left))

    def second_hop_sent():
        for number, (slot, rows) in ((4, (left, first)), (5, (right, second))):
            remote(
                vals.at[slot, rows], vals.at[slot, rows], v_ssem.at[number], v_rsem.at[number], at(y=left)
            ).wait_send()

    theirs = pl.ds(pl.multiple_of((1 - core) * HALF, HALF), HALF)
    ours = pl.ds(pl.multiple_of(core * HALF, HALF), HALF)
    for h in range(LOCAL_HEADS):
        for copy in loads[h]:
            copy.wait()
        part[h] = lax.dot_general(
            q_v[h].reshape(ROWS_HERE * HEAD_DIM, COLS),
            k_v[h].reshape(ROWS_HERE * HEAD_DIM, COLS),
            (((0,), (0,)), ((), ())),
            preferred_element_type=jnp.float32,
        )
        started.append(send(part.at[h, theirs], c_recv.at[h], c_ssem.at[h], c_rsem.at[h], mate))
        if h == 0:
            meet(0)
    meet(1)

    for h in range(LOCAL_HEADS):
        arrived(c_recv.at[h], c_rsem.at[h])
        csum[h] = (part[h, ours, :] + c_recv[h]).reshape(NX, XROWS, COLS)
        for d in (2, 1, 3):
            other = turn(x, d, NX)
            started.append(send(
                csum.at[h, other], x_recv.at[h, x], x_ssem.at[h, d], x_rsem.at[h, x], at(x=other)
            ))
        if h == 0:
            send_values(2, second, right)
            send_values(3, first, left)
            meet(2)
    meet(3)


    def owner_of(h, t):
        return lax.rem(t * 4 + h + NZ - 2 * core, NZ)

    for h in range(LOCAL_HEADS):
        total = csum[h, x]
        for d in range(1, NX):
            other = turn(x, d, NX)
            arrived(x_recv.at[h, other], x_rsem.at[h, other])
            total = total + x_recv[h, other]
        xsum[h] = total.reshape(GROUPS, 8, COLS)
        for t in range(GROUPS):
            owner = owner_of(h, t)

            @pl.when(owner != z)
            def _():
                send(xsum.at[h, t], z_recv.at[z], z_ssem.at[h, t], z_rsem.at[z], at(z=owner))

            @pl.when(owner == z)
            def _():
                z_recv[z] = xsum[h, t]

    turned = turn(z, 2 * core, NZ)
    kind, group = lax.rem(turned, 4), turned // 4
    owns = kind < LOCAL_HEADS
    here = core * NX + x

    def same_kind():
        return [
            (dy, dz, at(y=turn(y, dy, NY), z=turn(z, 4 * dz, NZ)))
            for dz in (2, 1, 3, 0) for dy in (2, 1, 3, 0) if dy or dz
        ]

    def bundle_targets():
        return [at(z=turn(z, 1, NZ)), at(z=turn(z, NZ - 1, NZ)), at(z=lax.rem(z + NZ - 2 + 4 * core, NZ))]

    def send_x(h):
        return [
            send(
                probs.at[h, :, here], probs.at[h, :, here],
                xg_ssem.at[h, d], xg_rsem.at[h, x], at(x=turn(x, d, NX)),
            )
            for d in (2, 1, 3)
        ]

    @pl.when(owns)
    def _():
        for d in range(1, NZ):
            other = turn(z, d, NZ)
            arrived(z_recv.at[other], z_rsem.at[other])
        logits = jnp.sum(z_recv[...], axis=0) * SCALING
        top = jnp.max(logits, axis=-1, keepdims=True)
        powers = jnp.exp(logits - top)
        p = powers / jnp.sum(powers, axis=-1, keepdims=True)
        pg[...] = jnp.concatenate([p[:, :128], p[:, 128:]], axis=0).astype(jnp.bfloat16)
        zg[group, y] = pg[...]
        for dy, dz, device in same_kind():
            send(pg, zg.at[group, y], zg_ssem.at[dz, dy], zg_rsem.at[group, y], device)

    second_hop()

    @pl.when(owns)
    def _():
        for dy, dz, _ in same_kind():
            slot = (turn(group, dz, 4), turn(y, dy, NY))
            arrived(zg.at[slot], zg_rsem.at[slot])
        for other_y in range(NY):
            blocks = []
            for t in range(GROUPS):
                block = zg[t, other_y].astype(jnp.float32)
                blocks.append(jnp.concatenate([block[:8], block[8:]], axis=1))
            probs[kind, other_y, here] = jnp.concatenate(blocks, axis=0).astype(jnp.bfloat16)
        for number, device in enumerate(bundle_targets()):
            send(
                probs.at[kind, :, here], probs.at[kind, :, here],
                z2_ssem.at[number], z2_rsem.at[kind], device,
            )
        send_x(kind)

    for step in (1, 3, 2):
        h = lax.rem(kind + step, 4)

        @pl.when(h < LOCAL_HEADS)
        def _():
            arrived(probs.at[h, :, here], z2_rsem.at[h])
            send_x(h)

    our_blocks = pl.ds(pl.multiple_of(core * NX, NX), NX)
    mate_blocks = pl.ds(pl.multiple_of((1 - core) * NX, NX), NX)
    for step in (0, 1, 3, 2):
        h = lax.rem(kind + step, 4)

        @pl.when(h < LOCAL_HEADS)
        def _():
            for d in range(1, NX):
                other = turn(x, d, NX)
                arrived(probs.at[h, :, core * NX + other], xg_rsem.at[h, other])
            send(probs.at[h, :, our_blocks], probs.at[h, :, our_blocks], cg_ssem.at[h], cg_rsem.at[h], mate)

    load_v.wait()
    load_w.wait()
    arrived(vals.at[left, second], v_rsem.at[2])
    arrived(vals.at[right, first], v_rsem.at[3])
    arrived(vals.at[far, first], v_rsem.at[4])
    arrived(vals.at[far, second], v_rsem.at[5])
    for h in range(LOCAL_HEADS):
        arrived(probs.at[h, :, mate_blocks], cg_rsem.at[h])
        features = pl.ds(h * HEAD_DIM, HEAD_DIM)
        for other_y in range(NY):
            attended = lax.dot_general(
                vals[other_y, :, features, :].reshape(ROWS_HERE * HEAD_DIM, COLS),
                probs[h, other_y].reshape(COLS, COLS),
                (((1,), (1,)), ((), ())),
                preferred_element_type=jnp.float32,
            )
            att[:, pl.ds(other_y * WIDTH_HERE + h * HEAD_DIM, HEAD_DIM), :] = (
                attended.astype(jnp.bfloat16).reshape(ROWS_HERE, HEAD_DIM, COLS)
            )

    for copy in started:
        copy.wait_send()
    second_hop_sent()
    for h in range(LOCAL_HEADS):
        remote(
            probs.at[h, :, our_blocks], probs.at[h, :, our_blocks], cg_ssem.at[h], cg_rsem.at[h], mate
        ).wait_send()
        for d in range(1, NX):
            remote(
                probs.at[h, :, here], probs.at[h, :, here],
                xg_ssem.at[h, d], xg_rsem.at[h, x], at(x=turn(x, d, NX)),
            ).wait_send()
        for t in range(GROUPS):
            owner = owner_of(h, t)

            @pl.when(owner != z)
            def _():
                remote(
                    xsum.at[h, t], z_recv.at[z], z_ssem.at[h, t], z_rsem.at[z], at(z=owner)
                ).wait_send()

    @pl.when(owns)
    def _():
        for dy, dz, device in same_kind():
            remote(pg, zg.at[group, y], zg_ssem.at[dz, dy], zg_rsem.at[group, y], device).wait_send()
        for number, device in enumerate(bundle_targets()):
            remote(
                probs.at[kind, :, here], probs.at[kind, :, here],
                z2_ssem.at[number], z2_rsem.at[kind], device,
            ).wait_send()


def project(att, w_v, out_hbm, out_v, out_sem):
    copies = []
    for r in range(ROWS_HERE):
        out_v[r] = jnp.dot(w_v[...], att[r], preferred_element_type=jnp.float32).astype(jnp.bfloat16)
        copies.append(pltpu.make_async_copy(out_v.at[r], out_hbm.at[r], out_sem.at[r]))
        copies[-1].start()
    for copy in copies:
        copy.wait()


def per_device(queries, keys, values, w_out):
    f32, bf16 = jnp.float32, jnp.bfloat16
    dma = pltpu.SemaphoreType.DMA
    whole = WIDTH_HERE * NY
    any_spec = pl.BlockSpec(memory_space=pl.ANY)
    vmem_spec = pl.BlockSpec(memory_space=pltpu.VMEM)
    attended, weights = pl.pallas_call(
        exchange,
        out_shape=(
            pltpu.VMEM((ROWS_HERE, whole, COLS), bf16),
            pltpu.VMEM((WIDTH_HERE, whole), bf16),
        ),
        in_specs=[pl.BlockSpec(memory_space=pltpu.HBM)] * 4,
        out_specs=(vmem_spec, vmem_spec),
        scratch_shapes=[
            pltpu.VMEM((LOCAL_HEADS, ROWS_HERE, HEAD_DIM, COLS), bf16),
            pltpu.VMEM((LOCAL_HEADS, ROWS_HERE, HEAD_DIM, COLS), bf16),
            pltpu.VMEM((NY, ROWS_HERE, WIDTH_HERE, COLS), bf16),
            pltpu.VMEM((LOCAL_HEADS, COLS, COLS), f32),
            pltpu.VMEM((LOCAL_HEADS, HALF, COLS), f32),
            pltpu.VMEM((LOCAL_HEADS, NX, XROWS, COLS), f32),
            pltpu.VMEM((LOCAL_HEADS, NX, XROWS, COLS), f32),
            pltpu.VMEM((LOCAL_HEADS, GROUPS, 8, COLS), f32),
            pltpu.VMEM((NZ, 8, COLS), f32),
            pltpu.VMEM((16, 128), bf16),
            pltpu.VMEM((GROUPS, NY, 16, 128), bf16),
            pltpu.VMEM((LOCAL_HEADS, NY, NC * NX, XROWS, COLS), bf16),
            dma((2 * LOCAL_HEADS + 2,)),
            pltpu.SemaphoreType.REGULAR((4,)),
            dma((6,)),
            dma((6,)),
            dma((LOCAL_HEADS,)),
            dma((LOCAL_HEADS,)),
            dma((LOCAL_HEADS, NX)),
            dma((LOCAL_HEADS, NX)),
            dma((LOCAL_HEADS, GROUPS)),
            dma((NZ,)),
            dma((4, NY)),
            dma((GROUPS, NY)),
            dma((3,)),
            dma((LOCAL_HEADS,)),
            dma((LOCAL_HEADS, NX)),
            dma((LOCAL_HEADS, NX)),
            dma((LOCAL_HEADS,)),
            dma((LOCAL_HEADS,)),
        ],
        compiler_params=pltpu.CompilerParams(
            collective_id=0, has_side_effects=True, vmem_limit_bytes=58 * 1024 * 1024
        ),
        cost_estimate=pl.CostEstimate(
            flops=1_500_000_000, bytes_accessed=4_000_000, transcendentals=2048
        ),
    )(queries, keys, values, w_out)
    return pl.pallas_call(
        project,
        out_shape=jax.ShapeDtypeStruct(values.shape, bf16),
        in_specs=[vmem_spec, vmem_spec],
        out_specs=any_spec,
        scratch_shapes=[pltpu.VMEM((ROWS_HERE, WIDTH_HERE, COLS), bf16), dma((ROWS_HERE,))],
        compiler_params=pltpu.CompilerParams(vmem_limit_bytes=16 * 1024 * 1024),
        cost_estimate=pl.CostEstimate(
            flops=906_000_000, bytes_accessed=6_000_000, transcendentals=0
        ),
    )(attended, weights)


def solution(mesh):
    return jax.shard_map(
        per_device,
        mesh=mesh,
        in_specs=(
            P("depth", "head", None),
            P("depth", "head", None),
            P("depth", "head", None),
            P("head", None),
        ),
        out_specs=P("depth", "head", None),
        check_vma=False,
    )
```

time: 72.8 us -> 58.5 us (0.80)
  Pallas kernels: 70.3 us -> 58.4 us
  local copies, waits for them, and re-layouts: 2.36 us -> 0 us
    pallas_call x1 -> x2, Pallas kernels: 70.3 us -> 58.4 us  [the longest x1 56.5 us: per_device(): pl.pallas_call(exchange, out_shape=(pltpu.VMEM((ROWS_HERE, whole, COLS),...]
    unnamed x1 -> x0, local copies, waits for them, and re-layouts: 2.36 us -> none
where the time goes in v2:
time: 58.5 us; the launch traced here: 58.4 us
  Pallas kernels  58.4 us (100%)
    pallas_call x1, Pallas kernels, per_device(): pl.pallas_call(exchange, out_shape=(pltpu.VMEM((ROWS_HERE, whole, COLS),...  56.5 us
    pallas_call x1, Pallas kernels, per_device(): pl.pallas_call(project, out_shape=jax.ShapeDtypeStruct(values.shape, bf16...  1.87 us

profile of v2, /device:TPU:1, one launch (start us, length us, event | category | flops | bytes accessed | tf_op | source)
XLA Modules:
  0.0 58.4 jit_solution(12532252028031988363)
XLA Ops:
  0.0 56.5 %shard_map.46 = (bf16[12,768,256]{2,1,0:T(8,128)(2,1)S(1)}, bf16[192,768]{1,0:T(8,128)(2,1)S(1)}) custom-call(bf16[12,192,256]{2,1,0:T(8,128)(2,1)} %q_hbm.1, bf16[12,192,256]{2,1,0:T(8,128)(2,1)} %k_hbm.1, bf16[12,192,256]{2,1,0:T(8,128)(2,1)} %v_hbm.1, bf16[192,768]{1,0:T(8,128)(2,1)} %w_hbm.1), custom_call_target="tpu_custom_call" | custom-call | flops 1500000000 | bytes 4000000 | tf_op jit(solution)/shard_map/pallas_call | solution.py:329
  56.5 1.9 %shard_map.47 = bf16[12,192,256]{2,1,0:T(8,128)(2,1)} custom-call(bf16[12,768,256]{2,1,0:T(8,128)(2,1)S(1)} %get-tuple-element.7.att, bf16[192,768]{1,0:T(8,128)(2,1)S(1)} %get-tuple-element.8.w_v), custom_call_target="tpu_custom_call" | custom-call | flops 906000000 | bytes 6000000 | tf_op jit(solution)/shard_map/pallas_call | solution.py:376

commit v3 on v2

v3 whole, which is shorter than its diff:
```python
import math

import jax
import jax.numpy as jnp
from jax import lax
from jax.experimental import pallas as pl
from jax.experimental.pallas import tpu as pltpu
from jax.sharding import PartitionSpec as P

HEAD_DIM = 64
NZ, NX, NY, NC = 16, 4, 4, 2
LOCAL_HEADS = 3
ROWS_HERE = 12
WIDTH_HERE = LOCAL_HEADS * HEAD_DIM
COLS = 256
HALF = COLS // NC
XROWS = HALF // NX
OWNERS = 12
GROUPS = XROWS // 8
HALF_SEQ = ROWS_HERE // 2
SCALING = 1.0 / math.sqrt(HEAD_DIM * ROWS_HERE * NZ * NX * NC)
MESH = pl.DeviceIdType.MESH


def exchange(
    q_hbm, k_hbm, v_hbm, w_hbm, att, w_v,
    q_v, k_v, vals, part, c_recv, csum, x_recv, xsum, z_recv, pg, packed, probs,
    load_sem, met_sem, v_ssem, v_rsem, c_ssem, c_rsem, x_ssem, x_rsem, z_ssem, z_rsem,
    zg_ssem, zg_rsem, z2_ssem, z2_rsem, xg_ssem, xg_rsem, cg_ssem, cg_rsem,
):
    me = lax.axis_index("depth")
    y = lax.axis_index("head")
    core = lax.rem(me, NC)
    x = lax.rem(me // NC, NX)
    z = me // (NC * NX)

    def at(z=z, x=x, core=core, y=y):
        return ((z * NX + x) * NC + core, y)

    def turn(index, by, size):
        return lax.rem(index + by, size)

    def remote(src, dst, ssem, rsem, device):
        return pltpu.make_async_remote_copy(
            src_ref=src, dst_ref=dst, send_sem=ssem, recv_sem=rsem,
            device_id=device, device_id_type=MESH,
        )

    def send(*args):
        copy = remote(*args)
        copy.start()
        return copy

    def arrived(dst, sem):
        remote(dst, dst, sem, sem, at()).wait_recv()

    load_q = pltpu.make_async_copy(q_hbm, q_v, load_sem.at[0])
    load_k = pltpu.make_async_copy(k_hbm, k_v, load_sem.at[1])
    load_q.start()
    load_k.start()

    rank = jnp.where(z < 8, z, jnp.where(z < 12, z + 4, 23 - z))

    mate = at(core=1 - core)
    barrier = pltpu.get_barrier_semaphore()
    near = (
        [at(y=turn(y, d, NY)) for d in range(1, NY)]
        + [mate]
        + [at(x=turn(x, d, NX)) for d in range(1, NX)]
    )

    def signal(semaphore, device):
        pl.semaphore_signal(semaphore, inc=1, device_id=device, device_id_type=MESH)

    for partner in near:
        signal(barrier, partner)

    def signal_ranks(semaphore, start, stop):
        @pl.loop(start, stop)
        def _(other):
            signal(semaphore, at(z=jnp.where(other < 8, other, jnp.where(other < 12, 23 - other, other - 4))))

    signal_ranks(barrier, rank + 1, NZ)
    load_v = pltpu.make_async_copy(v_hbm, vals.at[y], load_sem.at[2])
    load_w = pltpu.make_async_copy(w_hbm, w_v, load_sem.at[3])

    started = []

    left, right, far = turn(y, NY - 1, NY), turn(y, 1, NY), turn(y, 2, NY)
    first, second = pl.ds(0, HALF_SEQ), pl.ds(HALF_SEQ, HALF_SEQ)

    def send_values(number, rows, target):
        started.append(send(
            v_hbm.at[rows], vals.at[y, rows], v_ssem.at[number], v_rsem.at[number], at(y=target)
        ))

    def second_hop():
        arrived(vals.at[left, first], v_rsem.at[0])
        send(vals.at[left, first], vals.at[left, first], v_ssem.at[4], v_rsem.at[4], at(y=right))
        arrived(vals.at[right, second], v_rsem.at[1])
        send(vals.at[right, second], vals.at[right, second], v_ssem.at[5], v_rsem.at[5], at(y=left))

    def second_hop_sent():
        for number, (slot, rows) in ((4, (left, first)), (5, (right, second))):
            remote(
                vals.at[slot, rows], vals.at[slot, rows], v_ssem.at[number], v_rsem.at[number], at(y=left)
            ).wait_send()

    theirs = pl.ds(pl.multiple_of((1 - core) * HALF, HALF), HALF)
    ours = pl.ds(pl.multiple_of(core * HALF, HALF), HALF)
    for h in range(LOCAL_HEADS):
        if h == 0:
            load_q.wait()
            load_k.wait()
        features = pl.ds(h * HEAD_DIM, HEAD_DIM)
        part[h] = lax.dot_general(
            q_v[:, features, :].reshape(ROWS_HERE * HEAD_DIM, COLS),
            k_v[:, features, :].reshape(ROWS_HERE * HEAD_DIM, COLS),
            (((0,), (0,)), ((), ())),
            preferred_element_type=jnp.float32,
        )
        if h == 0:
            pl.semaphore_wait(barrier, len(near) + rank)
        started.append(send(part.at[h, theirs], c_recv.at[h], c_ssem.at[h], c_rsem.at[h], mate))
        if h == 0:
            send_values(0, first, right)
            send_values(1, second, left)

    @pl.when(rank < OWNERS)
    def _():
        signal_ranks(met_sem, 0, rank)

    for h in range(LOCAL_HEADS):
        arrived(c_recv.at[h], c_rsem.at[h])
        csum[h] = (part[h, ours, :] + c_recv[h]).reshape(NX, XROWS, COLS)
        for d in (2, 1, 3):
            other = turn(x, d, NX)
            started.append(send(
                csum.at[h, other], x_recv.at[h, x], x_ssem.at[h, d], x_rsem.at[h, x], at(x=other)
            ))


    def owner_of(h, t):
        return lax.rem(20 - 4 * h + t, NZ)

    load_v.start()
    load_w.start()
    @pl.when(rank < OWNERS - 1)
    def _():
        pl.semaphore_wait(met_sem, OWNERS - 1 - rank)

    for h in range(LOCAL_HEADS):
        total = csum[h, x]
        for d in range(1, NX):
            other = turn(x, d, NX)
            arrived(x_recv.at[h, other], x_rsem.at[h, other])
            total = total + x_recv[h, other]
        xsum[h] = total.reshape(GROUPS, 8, COLS)
        for t in range(GROUPS):
            owner = owner_of(h, t)

            @pl.when(owner != z)
            def _():
                send(xsum.at[h, t], z_recv.at[z], z_ssem.at[h, t], z_rsem.at[z], at(z=owner))

            @pl.when(owner == z)
            def _():
                z_recv[z] = xsum[h, t]
    send_values(2, second, right)
    send_values(3, first, left)

    own_head, kind = lax.rem(NZ + 1 - z // 4, 4), lax.rem(z, 4)
    owns = own_head < LOCAL_HEADS
    here = core * NX + x

    def each_first(act):
        for number in (0, 1, 3, 2):
            other = 4 * number + kind
            for dy in (2, 1, 3):
                act(number, dy, at(y=turn(y, dy, NY), z=other))

            @pl.when(other != z)
            def _():
                act(number, 0, at(z=other))

    half, place = y // 2, lax.rem(y, 2)

    def first_copy(number, dy, device):
        return remote(
            pg, packed.at[half, here, kind, own_head, place],
            zg_ssem.at[number, dy], zg_rsem.at[own_head, y], device,
        )

    our_blocks = pl.ds(pl.multiple_of(core * NX, NX), NX)
    mate_blocks = pl.ds(pl.multiple_of((1 - core) * NX, NX), NX)

    def each_z(act):
        targets = (
            (turn(z, 1, NZ), z < NZ - 1),
            (turn(z, NZ - 1, NZ), z >= 0),
            (lax.rem(z + NZ - 2 + 4 * core, NZ), jnp.logical_or(core == 0, z < NZ - 2)),
            (0, z == 3),
            (jnp.maximum(z - 2, 0), jnp.logical_and(core == 1, z // 2 == 1)),
        )
        for number, (target, there) in enumerate(targets):
            @pl.when(there)
            def _():
                act(remote(
                    packed.at[:, here, kind], packed.at[:, here, kind],
                    z2_ssem.at[number], z2_rsem.at[kind], at(z=target),
                ))

    def x_copies(t):
        return [
            remote(
                packed.at[:, here, t], packed.at[:, here, t],
                xg_ssem.at[t, d], xg_rsem.at[t, x], at(x=turn(x, d, NX)),
            )
            for d in (2, 1, 3)
        ]

    def core_copy(t):
        return remote(
            packed.at[:, our_blocks, t], packed.at[:, our_blocks, t], cg_ssem.at[t], cg_rsem.at[t], mate
        )

    @pl.when(owns)
    def _():
        for d in range(1, NZ):
            other = turn(z, d, NZ)
            arrived(z_recv.at[other], z_rsem.at[other])
        logits = jnp.sum(z_recv[...], axis=0) * SCALING
        top = jnp.max(logits, axis=-1, keepdims=True)
        powers = jnp.exp(logits - top)
        p = powers / jnp.sum(powers, axis=-1, keepdims=True)
        pg[...] = jnp.concatenate([p[:, :128], p[:, 128:]], axis=0).astype(jnp.bfloat16)
        packed[half, here, kind, own_head, place] = pg[...]
        each_first(lambda *where: first_copy(*where).start())

    second_hop()

    for h in range(LOCAL_HEADS):
        for dy in range(1, NY):
            other = turn(y, dy, NY)
            arrived(packed.at[other // 2, here, kind, h, lax.rem(other, 2)], zg_rsem.at[h, other])

        @pl.when(own_head != h)
        def _():
            arrived(packed.at[half, here, kind, h, place], zg_rsem.at[h, y])

    def start(copies):
        for copy in copies:
            copy.start()

    others = [turn(kind, d, 4) for d in (1, 3, 2)]
    each_z(lambda copy: copy.start())
    start(x_copies(kind))
    for t in others:
        arrived(packed.at[:, here, t], z2_rsem.at[t])
        start(x_copies(t))
    for t in [kind] + others:
        for d in range(1, NX):
            other = turn(x, d, NX)
            arrived(packed.at[:, core * NX + other, t], xg_rsem.at[t, other])
        core_copy(t).start()

    def unpack(which):
        @pl.loop(0, LOCAL_HEADS * NY)
        def _(number):
            h, other_y = number // NY, lax.rem(number, NY)
            for b in range(NX):
                blocks = packed[other_y // 2, which * NX + b, :, h, lax.rem(other_y, 2)].astype(jnp.float32)
                probs[h, other_y, which * NX + b] = jnp.concatenate(
                    [blocks[:, :8].reshape(XROWS, 128), blocks[:, 8:].reshape(XROWS, 128)], axis=1
                ).astype(jnp.bfloat16)

    unpack(core)
    load_v.wait()
    load_w.wait()
    for copy in started:
        copy.wait_send()
    second_hop_sent()
    for h in range(LOCAL_HEADS):
        for t in range(GROUPS):
            owner = owner_of(h, t)

            @pl.when(owner != z)
            def _():
                remote(
                    xsum.at[h, t], z_recv.at[z], z_ssem.at[h, t], z_rsem.at[z], at(z=owner)
                ).wait_send()

    @pl.when(owns)
    def _():
        each_first(lambda *where: first_copy(*where).wait_send())

    each_z(lambda copy: copy.wait_send())
    for t in range(GROUPS):
        for copy in x_copies(t):
            copy.wait_send()
        core_copy(t).wait_send()
    arrived(vals.at[left, second], v_rsem.at[2])
    arrived(vals.at[right, first], v_rsem.at[3])
    arrived(vals.at[far, first], v_rsem.at[4])
    arrived(vals.at[far, second], v_rsem.at[5])
    for t in [kind] + others:
        arrived(packed.at[:, mate_blocks, t], cg_rsem.at[t])
    unpack(1 - core)
    for h in range(LOCAL_HEADS):
        features = pl.ds(h * HEAD_DIM, HEAD_DIM)
        for other_y in range(NY):
            attended = lax.dot_general(
                vals[other_y, :, features, :].reshape(ROWS_HERE * HEAD_DIM, COLS),
                probs[h, other_y].reshape(COLS, COLS),
                (((1,), (1,)), ((), ())),
                preferred_element_type=jnp.float32,
            )
            att[:, pl.ds(other_y * WIDTH_HERE + h * HEAD_DIM, HEAD_DIM), :] = (
                attended.astype(jnp.bfloat16).reshape(ROWS_HERE, HEAD_DIM, COLS)
            )


def project(att, w_v, out_hbm, out_v, out_sem):
    copies = []
    for r in range(ROWS_HERE):
        out_v[r] = jnp.dot(w_v[...], att[r], preferred_element_type=jnp.float32).astype(jnp.bfloat16)
        copies.append(pltpu.make_async_copy(out_v.at[r], out_hbm.at[r], out_sem.at[r]))
        copies[-1].start()
    for copy in copies:
        copy.wait()


def per_device(queries, keys, values, w_out):
    f32, bf16 = jnp.float32, jnp.bfloat16
    dma = pltpu.SemaphoreType.DMA
    whole = WIDTH_HERE * NY
    any_spec = pl.BlockSpec(memory_space=pl.ANY)
    vmem_spec = pl.BlockSpec(memory_space=pltpu.VMEM)
    attended, weights = pl.pallas_call(
        exchange,
        out_shape=(
            pltpu.VMEM((ROWS_HERE, whole, COLS), bf16),
            pltpu.VMEM((WIDTH_HERE, whole), bf16),
        ),
        in_specs=[pl.BlockSpec(memory_space=pltpu.HBM)] * 4,
        out_specs=(vmem_spec, vmem_spec),
        scratch_shapes=[
            pltpu.VMEM((ROWS_HERE, WIDTH_HERE, COLS), bf16),
            pltpu.VMEM((ROWS_HERE, WIDTH_HERE, COLS), bf16),
            pltpu.VMEM((NY, ROWS_HERE, WIDTH_HERE, COLS), bf16),
            pltpu.VMEM((LOCAL_HEADS, COLS, COLS), f32),
            pltpu.VMEM((LOCAL_HEADS, HALF, COLS), f32),
            pltpu.VMEM((LOCAL_HEADS, NX, XROWS, COLS), f32),
            pltpu.VMEM((LOCAL_HEADS, NX, XROWS, COLS), f32),
            pltpu.VMEM((LOCAL_HEADS, GROUPS, 8, COLS), f32),
            pltpu.VMEM((NZ, 8, COLS), f32),
            pltpu.VMEM((16, 128), bf16),
            pltpu.VMEM((2, NC * NX, GROUPS, LOCAL_HEADS, NY // 2, 16, 128), bf16),
            pltpu.VMEM((LOCAL_HEADS, NY, NC * NX, XROWS, COLS), bf16),
            dma((4,)),
            pltpu.SemaphoreType.REGULAR,
            dma((6,)),
            dma((6,)),
            dma((LOCAL_HEADS,)),
            dma((LOCAL_HEADS,)),
            dma((LOCAL_HEADS, NX)),
            dma((LOCAL_HEADS, NX)),
            dma((LOCAL_HEADS, GROUPS)),
            dma((NZ,)),
            dma((4, NY)),
            dma((LOCAL_HEADS, NY)),
            dma((5,)),
            dma((GROUPS,)),
            dma((GROUPS, NX)),
            dma((GROUPS, NX)),
            dma((GROUPS,)),
            dma((GROUPS,)),
        ],
        compiler_params=pltpu.CompilerParams(
            collective_id=0, has_side_effects=True, vmem_limit_bytes=58 * 1024 * 1024
        ),
        cost_estimate=pl.CostEstimate(
            flops=1_500_000_000, bytes_accessed=4_000_000, transcendentals=2048
        ),
    )(queries, keys, values, w_out)
    return pl.pallas_call(
        project,
        out_shape=jax.ShapeDtypeStruct(values.shape, bf16),
        in_specs=[vmem_spec, vmem_spec],
        out_specs=any_spec,
        scratch_shapes=[pltpu.VMEM((ROWS_HERE, WIDTH_HERE, COLS), bf16), dma((ROWS_HERE,))],
        compiler_params=pltpu.CompilerParams(vmem_limit_bytes=16 * 1024 * 1024),
        cost_estimate=pl.CostEstimate(
            flops=906_000_000, bytes_accessed=6_000_000, transcendentals=0
        ),
    )(attended, weights)


def solution(mesh):
    return jax.shard_map(
        per_device,
        mesh=mesh,
        in_specs=(
            P("depth", "head", None),
            P("depth", "head", None),
            P("depth", "head", None),
            P("head", None),
        ),
        out_specs=P("depth", "head", None),
        check_vma=False,
    )
```

time: 58.5 us -> 56.1 us (0.959)
  Pallas kernels: 58.4 us -> 56 us
    pallas_call x1, Pallas kernels: 56.5 us -> 54.1 us  [per_device(): pl.pallas_call(exchange, out_shape=(pltpu.VMEM((ROWS_HERE, whole, COLS),...]
where the time goes in v3:
time: 56.1 us; the launch traced here: 56 us
  Pallas kernels  56 us (100%)
    pallas_call x1, Pallas kernels, per_device(): pl.pallas_call(exchange, out_shape=(pltpu.VMEM((ROWS_HERE, whole, COLS),...  54.1 us
    pallas_call x1, Pallas kernels, per_device(): pl.pallas_call(project, out_shape=jax.ShapeDtypeStruct(values.shape, bf16...  1.87 us

profile of v3, /device:TPU:1, one launch (start us, length us, event | category | flops | bytes accessed | tf_op | source)
XLA Modules:
  0.0 56.0 jit_solution(2766693145209859864)
XLA Ops:
  0.0 54.1 %shard_map.46 = (bf16[12,768,256]{2,1,0:T(8,128)(2,1)S(1)}, bf16[192,768]{1,0:T(8,128)(2,1)S(1)}) custom-call(bf16[12,192,256]{2,1,0:T(8,128)(2,1)} %q_hbm.1, bf16[12,192,256]{2,1,0:T(8,128)(2,1)} %k_hbm.1, bf16[12,192,256]{2,1,0:T(8,128)(2,1)} %v_hbm.1, bf16[192,768]{1,0:T(8,128)(2,1)} %w_hbm.1), custom_call_target="tpu_custom_call" | custom-call | flops 1500000000 | bytes 4000000 | tf_op jit(solution)/shard_map/pallas_call | solution.py:339
  54.1 1.9 %shard_map.47 = bf16[12,192,256]{2,1,0:T(8,128)(2,1)} custom-call(bf16[12,768,256]{2,1,0:T(8,128)(2,1)S(1)} %get-tuple-element.7.att, bf16[192,768]{1,0:T(8,128)(2,1)S(1)} %get-tuple-element.8.w_v), custom_call_target="tpu_custom_call" | custom-call | flops 906000000 | bytes 6000000 | tf_op jit(solution)/shard_map/pallas_call | solution.py:386

commit v4 on v3

--- a/solution.py
+++ b/solution.py
@@ -75,12 +75,26 @@
     for partner in near:
         signal(barrier, partner)
 
-    def signal_ranks(semaphore, start, stop):
+    def z_of(other):
+        return jnp.where(other < 8, other, jnp.where(other < 12, 23 - other, other - 4))
+
+    def apart(a, b):
+        za, zb = z_of(a), z_of(b)
+        late = jnp.logical_and(a >= 8, za - zb > 4)
+        mixed = jnp.logical_and(a // 2 == 3, jnp.logical_and(b >= 8, b < 11))
+        return jnp.logical_or(late, mixed)
+
+    def signal_ranks(semaphore, start, stop, far):
         @pl.loop(start, stop)
         def _(other):
-            signal(semaphore, at(z=jnp.where(other < 8, other, jnp.where(other < 12, 23 - other, other - 4))))
-
-    signal_ranks(barrier, rank + 1, NZ)
+            held_back = apart(jnp.minimum(rank, other), jnp.maximum(rank, other))
+
+            @pl.when(held_back if far else jnp.logical_not(held_back))
+            def _():
+                signal(semaphore, at(z=z_of(other)))
+
+    later = jnp.where(jnp.logical_and(z >= 8, z < 11), 11 - z, jnp.where(z >= 13, 2, 0))
+    signal_ranks(barrier, rank + 1, NZ, False)
     load_v = pltpu.make_async_copy(v_hbm, vals.at[y], load_sem.at[2])
     load_w = pltpu.make_async_copy(w_hbm, w_v, load_sem.at[3])
 
@@ -120,7 +134,7 @@
             preferred_element_type=jnp.float32,
         )
         if h == 0:
-            pl.semaphore_wait(barrier, len(near) + rank)
+            pl.semaphore_wait(barrier, len(near) + rank - later)
         started.append(send(part.at[h, theirs], c_recv.at[h], c_ssem.at[h], c_rsem.at[h], mate))
         if h == 0:
             send_values(0, first, right)
@@ -128,7 +142,12 @@
 
     @pl.when(rank < OWNERS)
     def _():
-        signal_ranks(met_sem, 0, rank)
+        signal_ranks(met_sem, 0, rank, False)
+
+    @pl.when(z == 11)
+    def _():
+        for d in range(1, 4):
+            signal(met_sem, at(z=z - d))
 
     for h in range(LOCAL_HEADS):
         arrived(c_recv.at[h], c_rsem.at[h])
@@ -145,9 +164,19 @@
 
     load_v.start()
     load_w.start()
+
+
     @pl.when(rank < OWNERS - 1)
     def _():
         pl.semaphore_wait(met_sem, OWNERS - 1 - rank)
+
+    @pl.when(z >= 13)
+    def _():
+        signal_ranks(met_sem, 6, 8, True)
+
+    @pl.when(jnp.logical_and(rank >= OWNERS, rank < NZ - 1))
+    def _():
+        pl.semaphore_wait(met_sem, 1)
 
     for h in range(LOCAL_HEADS):
         total = csum[h, x]
@@ -173,23 +202,25 @@
     owns = own_head < LOCAL_HEADS
     here = core * NX + x
 
+    half, place = y // 2, lax.rem(y, 2)
+
     def each_first(act):
-        for number in (0, 1, 3, 2):
+        def first_copy(number, dy, device, sem):
+            act(remote(pg, packed.at[half, here, kind, own_head, place], zg_ssem.at[number, dy], sem, device))
+
+        @pl.when(kind > 0)
+        def _():
+            for dy in range(NY):
+                first_copy(4, dy, at(y=turn(y, dy, NY), z=0), z2_rsem.at[kind])
+
+        for number in (0, 3, 1, 2):
             other = 4 * number + kind
             for dy in (2, 1, 3):
-                act(number, dy, at(y=turn(y, dy, NY), z=other))
+                first_copy(number, dy, at(y=turn(y, dy, NY), z=other), zg_rsem.at[own_head, y])
 
             @pl.when(other != z)
             def _():
-                act(number, 0, at(z=other))
-
-    half, place = y // 2, lax.rem(y, 2)
-
-    def first_copy(number, dy, device):
-        return remote(
-            pg, packed.at[half, here, kind, own_head, place],
-            zg_ssem.at[number, dy], zg_rsem.at[own_head, y], device,
-        )
+                first_copy(number, 0, at(z=other), zg_rsem.at[own_head, y])
 
     our_blocks = pl.ds(pl.multiple_of(core * NX, NX), NX)
     mate_blocks = pl.ds(pl.multiple_of((1 - core) * NX, NX), NX)
@@ -197,10 +228,9 @@
     def each_z(act):
         targets = (
             (turn(z, 1, NZ), z < NZ - 1),
-            (turn(z, NZ - 1, NZ), z >= 0),
-            (lax.rem(z + NZ - 2 + 4 * core, NZ), jnp.logical_or(core == 0, z < NZ - 2)),
-            (0, z == 3),
-            (jnp.maximum(z - 2, 0), jnp.logical_and(core == 1, z // 2 == 1)),
+            (turn(z, NZ - 1, NZ), z != 1),
+            (lax.rem(z + NZ - 2 + 4 * core, NZ), jnp.where(core == 0, z != 2, z < NZ - 2)),
+            (1, jnp.logical_and(core == 1, z == 3)),
         )
         for number, (target, there) in enumerate(targets):
             @pl.when(there)
@@ -235,7 +265,7 @@
         p = powers / jnp.sum(powers, axis=-1, keepdims=True)
         pg[...] = jnp.concatenate([p[:, :128], p[:, 128:]], axis=0).astype(jnp.bfloat16)
         packed[half, here, kind, own_head, place] = pg[...]
-        each_first(lambda *where: first_copy(*where).start())
+        each_first(lambda copy: copy.start())
 
     second_hop()
 
@@ -252,7 +282,7 @@
         for copy in copies:
             copy.start()
 
-    others = [turn(kind, d, 4) for d in (1, 3, 2)]
+    others = [turn(kind, jnp.where(z == 0, a, b), 4) for a, b in ((1, 3), (2, 1), (3, 2))]
     each_z(lambda copy: copy.start())
     start(x_copies(kind))
     for t in others:
@@ -292,7 +322,7 @@
 
     @pl.when(owns)
     def _():
-        each_first(lambda *where: first_copy(*where).wait_send())
+        each_first(lambda copy: copy.wait_send())
 
     each_z(lambda copy: copy.wait_send())
     for t in range(GROUPS):
@@ -367,9 +397,9 @@
             dma((LOCAL_HEADS, NX)),
             dma((LOCAL_HEADS, GROUPS)),
             dma((NZ,)),
-            dma((4, NY)),
+            dma((5, NY)),
             dma((LOCAL_HEADS, NY)),
-            dma((5,)),
+            dma((4,)),
             dma((GROUPS,)),
             dma((GROUPS, NX)),
             dma((GROUPS, NX)),

time: 56.1 us -> 53.3 us (0.950)
  Pallas kernels: 56 us -> 52.8 us
    pallas_call x1, Pallas kernels: 54.1 us -> 50.9 us  [per_device(): pl.pallas_call(exchange, out_shape=(pltpu.VMEM((ROWS_HERE, whole, COLS),...]
where the time goes in v4:
time: 53.3 us; the launch traced here: 52.8 us
  Pallas kernels  52.8 us (99%)
    pallas_call x1, Pallas kernels, per_device(): pl.pallas_call(exchange, out_shape=(pltpu.VMEM((ROWS_HERE, whole, COLS),...  50.9 us
    pallas_call x1, Pallas kernels, per_device(): pl.pallas_call(project, out_shape=jax.ShapeDtypeStruct(values.shape, bf16...  1.87 us

profile of v4, /device:TPU:1, one launch (start us, length us, event | category | flops | bytes accessed | tf_op | source)
XLA Modules:
  0.0 52.8 jit_solution(1577221667371448356)
XLA Ops:
  0.0 50.9 %shard_map.46 = (bf16[12,768,256]{2,1,0:T(8,128)(2,1)S(1)}, bf16[192,768]{1,0:T(8,128)(2,1)S(1)}) custom-call(bf16[12,192,256]{2,1,0:T(8,128)(2,1)} %q_hbm.1, bf16[12,192,256]{2,1,0:T(8,128)(2,1)} %k_hbm.1, bf16[12,192,256]{2,1,0:T(8,128)(2,1)} %v_hbm.1, bf16[192,768]{1,0:T(8,128)(2,1)} %w_hbm.1), custom_call_target="tpu_custom_call" | custom-call | flops 1500000000 | bytes 4000000 | tf_op jit(solution)/shard_map/pallas_call | solution.py:369
  50.9 1.9 %shard_map.47 = bf16[12,192,256]{2,1,0:T(8,128)(2,1)} custom-call(bf16[12,768,256]{2,1,0:T(8,128)(2,1)S(1)} %get-tuple-element.7.att, bf16[192,768]{1,0:T(8,128)(2,1)S(1)} %get-tuple-element.8.w_v), custom_call_target="tpu_custom_call" | custom-call | flops 906000000 | bytes 6000000 | tf_op jit(solution)/shard_map/pallas_call | solution.py:416

commit v5 on v4

--- a/solution.py
+++ b/solution.py
@@ -294,17 +294,16 @@
             arrived(packed.at[:, core * NX + other, t], xg_rsem.at[t, other])
         core_copy(t).start()
 
-    def unpack(which):
-        @pl.loop(0, LOCAL_HEADS * NY)
-        def _(number):
-            h, other_y = number // NY, lax.rem(number, NY)
-            for b in range(NX):
-                blocks = packed[other_y // 2, which * NX + b, :, h, lax.rem(other_y, 2)].astype(jnp.float32)
-                probs[h, other_y, which * NX + b] = jnp.concatenate(
-                    [blocks[:, :8].reshape(XROWS, 128), blocks[:, 8:].reshape(XROWS, 128)], axis=1
-                ).astype(jnp.bfloat16)
-
-    unpack(core)
+    def unpack(which, h, other_y):
+        for b in range(NX):
+            blocks = packed[other_y // 2, which * NX + b, :, h, other_y % 2].astype(jnp.float32)
+            probs[h, other_y, which * NX + b] = jnp.concatenate(
+                [blocks[:, :8].reshape(XROWS, 128), blocks[:, 8:].reshape(XROWS, 128)], axis=1
+            ).astype(jnp.bfloat16)
+
+    for h in range(LOCAL_HEADS):
+        for other_y in range(NY):
+            unpack(core, h, other_y)
     load_v.wait()
     load_w.wait()
     for copy in started:
@@ -335,10 +334,10 @@
     arrived(vals.at[far, second], v_rsem.at[5])
     for t in [kind] + others:
         arrived(packed.at[:, mate_blocks, t], cg_rsem.at[t])
-    unpack(1 - core)
     for h in range(LOCAL_HEADS):
         features = pl.ds(h * HEAD_DIM, HEAD_DIM)
         for other_y in range(NY):
+            unpack(1 - core, h, other_y)
             attended = lax.dot_general(
                 vals[other_y, :, features, :].reshape(ROWS_HERE * HEAD_DIM, COLS),
                 probs[h, other_y].reshape(COLS, COLS),

time: 53.3 us -> 53.2 us (level)
  no operation moved by 1% of the time
where the time goes in v5:
time: 53.2 us; the launch traced here: 52.6 us
  Pallas kernels  52.6 us (99%)
    pallas_call x1, Pallas kernels, per_device(): pl.pallas_call(exchange, out_shape=(pltpu.VMEM((ROWS_HERE, whole, COLS),...  50.8 us
    pallas_call x1, Pallas kernels, per_device(): pl.pallas_call(project, out_shape=jax.ShapeDtypeStruct(values.shape, bf16...  1.87 us

profile of v5, /device:TPU:1, one launch (start us, length us, event | category | flops | bytes accessed | tf_op | source)
XLA Modules:
  0.0 52.6 jit_solution(8222483404046255159)
XLA Ops:
  0.0 50.8 %shard_map.46 = (bf16[12,768,256]{2,1,0:T(8,128)(2,1)S(1)}, bf16[192,768]{1,0:T(8,128)(2,1)S(1)}) custom-call(bf16[12,192,256]{2,1,0:T(8,128)(2,1)} %q_hbm.1, bf16[12,192,256]{2,1,0:T(8,128)(2,1)} %k_hbm.1, bf16[12,192,256]{2,1,0:T(8,128)(2,1)} %v_hbm.1, bf16[192,768]{1,0:T(8,128)(2,1)} %w_hbm.1), custom_call_target="tpu_custom_call" | custom-call | flops 1500000000 | bytes 4000000 | tf_op jit(solution)/shard_map/pallas_call | solution.py:368
  50.8 1.9 %shard_map.47 = bf16[12,192,256]{2,1,0:T(8,128)(2,1)} custom-call(bf16[12,768,256]{2,1,0:T(8,128)(2,1)S(1)} %get-tuple-element.7.att, bf16[192,768]{1,0:T(8,128)(2,1)S(1)} %get-tuple-element.8.w_v), custom_call_target="tpu_custom_call" | custom-call | flops 906000000 | bytes 6000000 | tf_op jit(solution)/shard_map/pallas_call | solution.py:415
